TPU v7x, 32 devices: a whole 2x2x4 slice. The times are simulated.
32 devices in a mesh: img: 32 (over z, y, x, core).
Axes of the slice: x: 2, y: 2, z: 4, core: 2. Of those that a mesh axis runs over, the one named last changes fastest.
Arguments:
- block_input: bfloat16 [448, 81, 2048], P('img'), may hold values from -8 to 8
- grid_side: int32 [448], P('img'), may hold values from 2 to 3
- tile_source: int32 [4032], P('img'), may hold values from 0 to 4031, as said below
- conv1_weight: bfloat16 [2048, 512], replicated, may hold values from -0.125 to 0.125
- gain1: float32 [512], replicated, may hold values from 0.5 to 1.5
- bias1: float32 [512], replicated, may hold values from -1.5 to 1.5
- conv2_weight: bfloat16 [9, 512, 512], replicated, may hold values from -0.09375 to 0.09375
- gain2: float32 [512], replicated, may hold values from 0.5 to 1.5
- bias2: float32 [512], replicated, may hold values from -1.5 to 1.5
- conv3_weight: bfloat16 [512, 2048], replicated, may hold values from -0.25 to 0.25
- gain3: float32 [2048], replicated, may hold values from 0.5 to 1.5
- bias3: float32 [2048], replicated, may hold values from -1.5 to 1.5
- head_weight: bfloat16 [2048, 128], replicated, may hold values from -0.125 to 0.125
- jigsaw_weight: bfloat16 [1152, 128], replicated, may hold values from -0.1875 to 0.1875
- out_cotangent: bfloat16 [448, 81, 2048], P('img'), may hold values from -6 to 6
- jigsaw_cotangent: bfloat16 [448, 128], P('img'), may hold values from -6 to 6
Outputs:
- block_output: bfloat16 [448, 81, 2048], P('img')
- jigsaw_output: float32 [448, 128], P('img')
- input_grad: bfloat16 [448, 81, 2048], P('img')
- conv1_grad: float32 [2048, 512], replicated
- gain1_grad: float32 [512], replicated
- bias1_grad: float32 [512], replicated
- conv2_grad: float32 [9, 512, 512], replicated
- gain2_grad: float32 [512], replicated
- bias2_grad: float32 [512], replicated
- conv3_grad: float32 [512, 2048], replicated
- gain3_grad: float32 [2048], replicated
- bias3_grad: float32 [2048], replicated
- head_grad: float32 [2048, 128], replicated
- jigsaw_grad: float32 [1152, 128], replicated
Inputs may be any that keep to these rules, and one draw needn't show every extreme that they name: The tile maps of image i use the upper left grid_side(i) x grid_side(i) pixels of the 3 x 3 slots. `tile_source`: entries 9 i to 9 i + 8 name each of image i's own tiles 9 i to 9 i + 8 exactly once.
All inputs are finite; a program needn't handle non-finite values.
Results may differ from a plain program's by a relative error of at most 0.0085.
Values sent between devices are 32-bit elements; how exact they have to be, the bound alone decides.
No kernel may reach another device: no remote copies, remote signals or barrier semaphores. Data moves between devices by JAX's collectives and lax.ppermute only.
A program may use at most 256 MiB of HBM per device.

v0:
```python
import jax
import jax.numpy as jnp
from jax import lax
from jax.sharding import PartitionSpec as P

epsilon = 1e-05
tap_offsets = ((-1, -1), (-1, 0), (-1, 1), (0, -1), (0, 0), (0, 1), (1, -1), (1, 0), (1, 1))


def tap_shift(maps, row_step, col_step):
    padded = jnp.pad(maps, ((0, 0), (1, 1), (1, 1), (0, 0)))
    return padded[:, 1 + row_step : 4 + row_step, 1 + col_step : 4 + col_step, :]


def gather_taps(values):
    width = values.shape[-1]
    maps = values.reshape(-1, 3, 3, width)
    pieces = [tap_shift(maps, offset[0], offset[1]) for offset in tap_offsets]
    return jnp.concatenate(pieces, axis=-1).reshape(-1, 9 * width)


def scatter_taps(columns, width):
    maps = columns.reshape(-1, 3, 3, 9 * width)
    total = jnp.zeros(maps.shape[:3] + (width,), jnp.float32)
    for index in range(9):
        row_step, col_step = tap_offsets[index]
        total = total + tap_shift(
            maps[..., index * width : (index + 1) * width], -row_step, -col_step
        )
    return total.reshape(-1, width)


def silu_slope(value):
    sigma = jax.nn.sigmoid(value)
    return sigma * (1.0 + value * (1.0 - sigma))


def statistics(value, mask, count_local):
    count, total = lax.psum((count_local, jnp.sum(value * mask, axis=0)), "img")
    mean = total / count
    centered = (value - mean) * mask
    spread = lax.psum(jnp.sum(centered * centered, axis=0), "img") / count
    return (count, mean, lax.rsqrt(spread + epsilon))


def normalize(value, mask, count_local, gain, bias, stored):
    stored = statistics(value, mask, count_local)
    hat = (value - stored[1]) * stored[2]
    return (gain * hat + bias, hat, stored)


def normalize_back(grad_norm, hat, gain, stored, mask):
    count, mean, scale = stored
    bias_grad, gain_grad = lax.psum(
        (jnp.sum(grad_norm, axis=0), jnp.sum(grad_norm * hat, axis=0)), "img"
    )
    grad_pre = mask * (scale * gain) * (grad_norm - bias_grad / count - hat * (gain_grad / count))
    return (grad_pre, gain_grad, bias_grad)


def block_forward(rows, mask, count_local, weights, stored):
    (
        first_weight,
        first_gain,
        first_bias,
        second_weight,
        second_gain,
        second_bias,
        third_weight,
        third_gain,
        third_bias,
    ) = weights
    width = first_weight.shape[1]
    pre_one = jnp.dot(rows, first_weight, preferred_element_type=jnp.float32)
    norm_one, hat_one, kept_one = normalize(
        pre_one, mask, count_local, first_gain, first_bias, stored[0]
    )
    act_one = (mask * jax.nn.silu(norm_one)).astype(jnp.bfloat16)
    columns = gather_taps(act_one)
    pre_two = jnp.dot(
        columns, second_weight.reshape(9 * width, width), preferred_element_type=jnp.float32
    )
    norm_two, hat_two, kept_two = normalize(
        pre_two, mask, count_local, second_gain, second_bias, stored[1]
    )
    act_two = (mask * jax.nn.silu(norm_two)).astype(jnp.bfloat16)
    pre_three = jnp.dot(act_two, third_weight, preferred_element_type=jnp.float32)
    norm_three, hat_three, kept_three = normalize(
        pre_three, mask, count_local, third_gain, third_bias, stored[2]
    )
    summed = norm_three + rows.astype(jnp.float32)
    output = mask * jax.nn.silu(summed)
    saved = (norm_one, hat_one, columns, norm_two, hat_two, act_two, hat_three, summed)
    return (output, saved, (kept_one, kept_two, kept_three))


def local(
    block_input,
    grid_side,
    tile_source,
    conv1_weight,
    gain1,
    bias1,
    conv2_weight,
    gain2,
    bias2,
    conv3_weight,
    gain3,
    bias3,
    head_weight,
    jigsaw_weight,
    out_cotangent,
    jigsaw_cotangent,
):
    images, slots, channels = block_input.shape
    embed = head_weight.shape[1]
    width = conv1_weight.shape[1]
    pixel = jnp.arange(9, dtype=jnp.int32)
    inside = ((pixel // 3)[None, :] < grid_side[:, None]) & (
        (pixel % 3)[None, :] < grid_side[:, None]
    )
    mask = jnp.broadcast_to(inside[:, None, :], (images, 9, 9)).reshape(-1, 1).astype(jnp.float32)
    count_local = jnp.sum(mask)
    area = jnp.repeat(1.0 / (grid_side * grid_side).astype(jnp.float32), 9)[:, None]
    rows = block_input.reshape(-1, channels) * mask.astype(jnp.bfloat16)
    weights = (conv1_weight, gain1, bias1, conv2_weight, gain2, bias2, conv3_weight, gain3, bias3)
    output, saved, kept = block_forward(rows, mask, count_local, weights, (None, None, None))
    pooled = (jnp.sum(output.reshape(-1, 9, channels), axis=1) * area).astype(jnp.bfloat16)
    embedded = jnp.dot(pooled, head_weight, preferred_element_type=jnp.float32).astype(jnp.bfloat16)
    local_source = (
        9 * jnp.arange(images, dtype=jnp.int32)[:, None] + tile_source.reshape(images, 9) % 9
    ).reshape(-1)
    joined = jnp.take(embedded, local_source, axis=0).reshape(images, 9 * embed)
    jigsaw_out = jnp.dot(joined, jigsaw_weight, preferred_element_type=jnp.float32)
    jigsaw_grad = jnp.einsum(
        "ik,ie->ke", joined, jigsaw_cotangent, preferred_element_type=jnp.float32
    )
    joined_grad = jnp.einsum(
        "ie,ke->ik", jigsaw_cotangent, jigsaw_weight, preferred_element_type=jnp.float32
    )
    embed_grad = (
        jnp.zeros((embedded.shape[0], embed), jnp.float32)
        .at[local_source]
        .add(joined_grad.reshape(-1, embed))
        .astype(jnp.bfloat16)
    )
    head_grad = jnp.einsum("tc,te->ce", pooled, embed_grad, preferred_element_type=jnp.float32)
    pooled_grad = jnp.einsum(
        "te,ce->tc", embed_grad, head_weight, preferred_element_type=jnp.float32
    )
    recomputed, saved, kept = block_forward(rows, mask, count_local, weights, (None, None, None))
    norm_one, hat_one, columns, norm_two, hat_two, act_two, hat_three, summed = saved
    spread_pool = jnp.broadcast_to(
        (pooled_grad * area)[:, None, :], (pooled_grad.shape[0], 9, channels)
    ).reshape(-1, channels)
    output_grad = out_cotangent.reshape(-1, channels).astype(jnp.float32) + mask * spread_pool
    summed_grad = output_grad * mask * silu_slope(summed)
    third_pre, gain3_grad, bias3_grad = normalize_back(summed_grad, hat_three, gain3, kept[2], mask)
    third_back = third_pre.astype(jnp.bfloat16)
    conv3_grad = jnp.einsum("rm,rc->mc", act_two, third_back, preferred_element_type=jnp.float32)
    act_two_grad = jnp.einsum(
        "rc,mc->rm", third_back, conv3_weight, preferred_element_type=jnp.float32
    )
    second_norm_grad = act_two_grad * mask * silu_slope(norm_two)
    second_pre, gain2_grad, bias2_grad = normalize_back(
        second_norm_grad, hat_two, gain2, kept[1], mask
    )
    second_back = second_pre.astype(jnp.bfloat16)
    conv2_grad = jnp.einsum(
        "rk,rm->km", columns, second_back, preferred_element_type=jnp.float32
    ).reshape(9, width, width)
    column_grad = jnp.einsum(
        "rm,km->rk",
        second_back,
        conv2_weight.reshape(9 * width, width),
        preferred_element_type=jnp.float32,
    )
    act_one_grad = scatter_taps(column_grad, width)
    first_norm_grad = act_one_grad * mask * silu_slope(norm_one)
    first_pre, gain1_grad, bias1_grad = normalize_back(
        first_norm_grad, hat_one, gain1, kept[0], mask
    )
    first_back = first_pre.astype(jnp.bfloat16)
    conv1_grad = jnp.einsum("rc,rm->cm", rows, first_back, preferred_element_type=jnp.float32)
    rows_grad = jnp.einsum(
        "rm,cm->rc", first_back, conv1_weight, preferred_element_type=jnp.float32
    )
    input_grad = (mask * (rows_grad + summed_grad)).astype(jnp.bfloat16).reshape(block_input.shape)
    conv1_grad, conv2_grad, conv3_grad, head_grad, jigsaw_grad = lax.psum(
        (conv1_grad, conv2_grad, conv3_grad, head_grad, jigsaw_grad), "img"
    )
    block_output = output.astype(jnp.bfloat16).reshape(block_input.shape)
    return (
        block_output,
        jigsaw_out,
        input_grad,
        conv1_grad,
        gain1_grad,
        bias1_grad,
        conv2_grad,
        gain2_grad,
        bias2_grad,
        conv3_grad,
        gain3_grad,
        bias3_grad,
        head_grad,
        jigsaw_grad,
    )


def solution(mesh):
    placed = (
        P("img", None, None),
        P("img"),
        P("img"),
        P(),
        P(),
        P(),
        P(),
        P(),
        P(),
        P(),
        P(),
        P(),
        P(),
        P(),
        P("img", None, None),
        P("img", None),
    )
    return jax.shard_map(
        local,
        mesh=mesh,
        in_specs=placed,
        out_specs=(
            P("img", None, None),
            P("img", None),
            P("img", None, None),
            P(),
            P(),
            P(),
            P(),
            P(),
            P(),
            P(),
            P(),
            P(),
            P(),
            P(),
        ),
        check_vma=False,
    )
```

profile of v0, /device:TPU:0, one launch (start us, length us, event | category | flops | bytes accessed | tf_op | source)
XLA Modules:
  0.0 994.1 jit_solution(178810714964457947)
XLA Ops:
  16.7 7.0 multiply_reduce_fusion.8
  23.7 42.2 %all-reduce.12 = (f32[512]{0:T(512)S(1)}, f32[]{:T(128)}) all-reduce(f32[512]{0:T(512)S(1)} %get-tuple-element.63, f32[]{:T(128)} %broadcast_reduce_fusion), channel_id=1, replica_groups=mesh['img'=32] {'img'}, use_global_device_ids=true, to_apply=%region_1.2 | all-reduce | flops 513 | bytes 4104 | tf_op jit(solution)/shard_map/psum | solution.py:39
  68.6 40.5 %psum.124 = f32[512]{0:T(512)S(1)} all-reduce(f32[512]{0:T(512)S(1)} %multiply_reduce_fusion.7), channel_id=1, replica_groups=mesh['img'=32] {'img'}, use_global_device_ids=true, to_apply=%region_5.6 | all-reduce | flops 512 | bytes 4096 | tf_op jit(solution)/shard_map/psum | solution.py:42
  114.8 8.9 reshape.205
  123.7 12.7 %pad_slice_fusion = (bf16[126,3,3,512]{3,2,1,0:T(4,128)(2,1)}, bf16[126,3,3,512]{3,2,1,0:T(4,128)(2,1)}, bf16[126,3,3,512]{3,2,1,0:T(4,128)(2,1)}, bf16[126,3,3,...) fusion(bf16[126,3,3,512]{3,2,1,0:T(4,128)(2,1)} %reshape.197), kind=kLoop, calls=%fused_computation.2 | loop fusion | bytes 10450944 | tf_op jit(solution)/shard_map/slice | solution.py:12
  173.3 10.7 %multiply_reduce_fusion.6 = (f32[512]{0:T(512)S(1)}, f32[1134,512]{1,0:T(8,128)}) fusion(f32[1134]{0:T(1024)S(1)} %convert_element_type.100, bf16[1134,4608]{1,0:T(8,128)(2,1)S(1)} %constant_dynamic-update-slice_fusion, bf16[4608,512]{1,0:T(8,128)(2,1)} %bitcast.36), kind=kOutput, calls=%fused_computation.52 | convolution fusion | flops 5352044032 | bytes 17498552 | tf_op jit(solution)/shard_map/dot_general | solution.py:80
  184.1 40.0 %psum.125 = f32[512]{0:T(512)S(1)} all-reduce(f32[512]{0:T(512)S(1)} %get-tuple-element.65), channel_id=1, replica_groups=mesh['img'=32] {'img'}, use_global_device_ids=true, to_apply=%region_7.8 | all-reduce | flops 512 | bytes 4096 | tf_op jit(solution)/shard_map/psum | solution.py:39
  226.7 40.1 %psum.126 = f32[512]{0:T(512)S(1)} all-reduce(f32[512]{0:T(512)S(1)} %multiply_reduce_fusion.5), channel_id=1, replica_groups=mesh['img'=32] {'img'}, use_global_device_ids=true, to_apply=%region_9.10 | all-reduce | flops 512 | bytes 4096 | tf_op jit(solution)/shard_map/psum | solution.py:42
  267.5 8.4 multiply_reduce_fusion.2
  275.9 40.0 %psum.129 = f32[2048]{0:T(1024)S(1)} all-reduce(f32[2048]{0:T(1024)S(1)} %get-tuple-element.67), channel_id=1, replica_groups=mesh['img'=32] {'img'}, use_global_device_ids=true, to_apply=%region_11.12 | all-reduce | flops 2048 | bytes 16384 | tf_op jit(solution)/shard_map/psum | solution.py:39
  316.6 5.0 multiply_reduce_fusion.1
  321.6 40.2 %psum.130 = f32[2048]{0:T(1024)S(1)} all-reduce(f32[2048]{0:T(1024)S(1)} %multiply_reduce_fusion.1), channel_id=1, replica_groups=mesh['img'=32] {'img'}, use_global_device_ids=true, to_apply=%region_13.14 | all-reduce | flops 2048 | bytes 16384 | tf_op jit(solution)/shard_map/psum | solution.py:42
  363.1 7.8 broadcast_in_dim.32
  370.9 11.5 %reshape.202 = f32[1134,2048]{1,0:T(8,128)} reshape(f32[126,9,2048]{2,1,0:T(8,128)} %broadcast_in_dim.32) | data formatting | bytes 18579456 | tf_op jit(solution)/shard_map/reshape | solution.py:155
  383.1 22.7 %fusion.35 = (f32[2048]{0:T(1024)S(1)}, f32[2048]{0:T(1024)S(1)}, f32[1134,2048]{1,0:T(8,128)}, bf16[1134,2048]{1,0:T(8,128)(2,1)}, f32[1134,2048]{1,0:T(8,128)}) fusion(f32[2048]{0:T(1024)S(1)} %get-tuple-element.39, f32[1134,2048]{1,0:T(8,128)} %get-tuple-element.68, f32[2048]{0:T(1024)S(1)} %broadcast_divide_fusion.2, bf16[1134,2048]{1,0:T(8,128)(2,1)} %reshape.196, ...), kind=kLoop, calls=%fused_computation.118 | loop fusion | flops 55734272 | bytes 55794324 | tf_op jit(solution)/shard_map/reduce_sum | solution.py:55
  405.7 40.0 %all-reduce.11 = (f32[2048]{0:T(1024)S(1)}, f32[2048]{0:T(1024)S(1)}) all-reduce(f32[2048]{0:T(1024)S(1)} %get-tuple-element.15, f32[2048]{0:T(1024)S(1)} %get-tuple-element.14), channel_id=1, replica_groups=mesh['img'=32] {'img'}, use_global_device_ids=true, to_apply=%region_19.20 | all-reduce | flops 4096 | bytes 32768 | tf_op jit(solution)/shard_map/psum | solution.py:54
  447.1 8.1 multiply_convert_fusion.1
  455.2 5.0 fusion.37
  464.9 10.9 %reshape.200 = f32[126,9,2048]{2,1,0:T(8,128)} reshape(f32[1134,2048]{1,0:T(8,128)} %get-tuple-element.54) | data formatting | bytes 18579456 | tf_op jit(solution)/shard_map/reshape | solution.py:128
  475.8 9.7 reduce_sum.134
  487.5 15.1 %copy.35 = bf16[4608,1134]{1,0:T(8,128)(2,1)} copy(bf16[4608,1134]{0,1:T(8,128)(2,1)} %bitcast.31) | data formatting | bytes 20901888 | tf_op jit(solution)/shard_map/rk,rm->km/dot_general | solution.py:169
  502.6 40.6 %all-reduce.10 = (f32[512]{0:T(512)S(1)}, f32[512]{0:T(512)S(1)}) all-reduce(f32[512]{0:T(512)S(1)} %get-tuple-element.19, f32[512]{0:T(512)S(1)} %get-tuple-element.18), channel_id=1, replica_groups=mesh['img'=32] {'img'}, use_global_device_ids=true, to_apply=%region_23.24 | all-reduce | flops 1024 | bytes 8192 | tf_op jit(solution)/shard_map/psum | solution.py:54
  549.4 12.7 %fusion.17 = f32[9,512,512]{2,1,0:T(8,128)} fusion(bf16[9,512,1134]{2,1,0:T(8,128)(2,1)} %bitcast.32, bf16[1134,512]{1,0:T(8,128)(2,1)S(1)} %multiply_convert_fusion.3), kind=kOutput, calls=%fused_computation.64 | convolution fusion | flops 5350883328 | bytes 21049344 | tf_op jit(solution)/shard_map/rk,rm->km/dot_general | solution.py:169
  562.8 12.3 %fusion.15 = f32[126,3,3,4608]{3,0,2,1:T(8,128)} fusion(bf16[4608,512,1,1]{1,0,3,2:T(8,128)(2,1)} %bitcast.37, bf16[126,3,3,512]{3,2,1,0:T(4,128)(2,1)} %dot_general.62), kind=kOutput, calls=%fused_computation.62 | convolution fusion | flops 5350883328 | bytes 26781696 | tf_op jit(solution)/shard_map/rm,km->rk/dot_general | solution.py:172
  575.1 9.1 fusion.42
  595.2 5.1 fusion.36
  600.3 39.8 %all-reduce.9 = (f32[512]{0:T(512)S(1)}, f32[512]{0:T(512)S(1)}) all-reduce(f32[512]{0:T(512)S(1)} %get-tuple-element.17, f32[512]{0:T(512)S(1)} %get-tuple-element.16), channel_id=1, replica_groups=mesh['img'=32] {'img'}, use_global_device_ids=true, to_apply=%region_27.28 | all-reduce | flops 1024 | bytes 8192 | tf_op jit(solution)/shard_map/psum | solution.py:54
  644.4 7.5 fusion.1
  657.9 10.4 %multiply_convert_fusion = bf16[1134,2048]{1,0:T(8,128)(2,1)} fusion(f32[1134,2048]{1,0:T(8,128)} %get-tuple-element.40, bf16[1134,512]{1,0:T(8,128)(2,1)S(1)} %multiply_convert_fusion.2, bf16[2048,512]{1,0:T(8,128)(2,1)} %param.19, f32[1134]{0:T(1024)S(1)} %convert_element_type.100), kind=kOutput, calls=%fused_computation.10 | convolution fusion | flops 2385137664 | bytes 17197496 | tf_op jit(solution)/shard_map/rm,cm->rc/dot_general | solution.py:185
  668.3 5.0 reshape.204
  674.1 294.9 %all-reduce.16.cloned.1.call-done = (f32[2048,512]{1,0:T(8,128)}, f32[9,512,512]{2,1,0:T(8,128)}, f32[512,2048]{1,0:T(8,128)}, f32[2048,128]{1,0:T(8,128)}, f32[1152,128]{1,0:T(8,128)}) async-done(((f32[2048,512]{1,0:T(8,128)}, f32[9,512,512]{2,1,0:T(8,128)}, f32[512,2048]{1,0:T(8,128)}, f32[2048,128]{1,0:T(8,128)}, f32[1152,128]{1,0:T(8,128)}), (f32[2048,512]{1,0:T(8,128)}, f32[9,512,512]{2,1,0:T(8,128)}, ...) | async-done | bytes 19464208 | tf_op jit(solution)/shard_map/psum | solution.py:189
  973.6 8.7 copy.56
  (136 shorter events, 106.9 us)
Async XLA Ops:
  7.2 260.3 %copy-start = (bf16[512,2048]{1,0:T(8,128)(2,1)S(1)}, bf16[512,2048]{1,0:T(8,128)(2,1)}, u32[]{:S(2)}) copy-start(bf16[512,2048]{1,0:T(8,128)(2,1)} %param.25) | copy-start | bytes 6291460
  7.2 961.8 %all-reduce.16.cloned.1.call-start = ((), (), s32[]{:S(2)}) async-start(), calls=%async_computation | async-start | bytes 38928384 | tf_op jit(solution)/shard_map/psum | solution.py:189
  23.7 85.4 %copy-start.17 = (f32[512]{0:T(512)S(1)}, f32[512]{0:T(512)}, u32[]{:S(2)}) copy-start(f32[512]{0:T(512)} %param.20) | copy-start | bytes 6148
  23.7 86.7 %copy-start.18 = (f32[512]{0:T(512)S(1)}, f32[512]{0:T(512)}, u32[]{:S(2)}) copy-start(f32[512]{0:T(512)} %param.21) | copy-start | bytes 6148
  166.9 1.6 copy-start.10
  166.9 2.0 copy-start.9
  168.5 1.4 copy-start.8
  168.8 1.7 copy-start.2
  170.6 1.3 copy-start.7
  170.6 1.6 copy-start.6
  171.8 1.4 copy-start.5
  173.3 10.7 %copy-start.3 = (bf16[1134,4608]{1,0:T(8,128)(2,1)}, bf16[1134,4608]{1,0:T(8,128)(2,1)S(1)}, u32[]{:S(2)}) copy-start(bf16[1134,4608]{1,0:T(8,128)(2,1)S(1)} %constant_dynamic-update-slice_fusion) | copy-start | bytes 31352836
  184.1 82.8 %copy-start.24 = (f32[512]{0:T(512)S(1)}, f32[512]{0:T(512)}, u32[]{:S(2)}) copy-start(f32[512]{0:T(512)} %param.23) | copy-start | bytes 6148
  184.1 83.5 %copy-start.29 = (f32[512]{0:T(512)S(1)}, f32[512]{0:T(512)}, u32[]{:S(2)}) copy-start(f32[512]{0:T(512)} %param.24) | copy-start | bytes 6148
  316.6 46.2 %copy-start.12 = (bf16[2048,128]{1,0:T(8,128)(2,1)S(1)}, bf16[2048,128]{1,0:T(8,128)(2,1)}, u32[]{:S(2)}) copy-start(bf16[2048,128]{1,0:T(8,128)(2,1)} %param.28) | copy-start | bytes 1572868
  370.9 11.5 %copy-start.16 = (f32[2048]{0:T(1024)S(1)}, f32[2048]{0:T(1024)}, u32[]{:S(2)}) copy-start(f32[2048]{0:T(1024)} %param.26) | copy-start | bytes 24580
  370.9 12.1 %copy-start.20 = (f32[2048]{0:T(1024)S(1)}, f32[2048]{0:T(1024)}, u32[]{:S(2)}) copy-start(f32[2048]{0:T(1024)} %param.27) | copy-start | bytes 24580
  445.8 9.4 copy-start.22
  445.8 9.4 copy-start.23
  447.1 8.1 copy-start.4
  543.1 4.3 copy-start.25
  543.1 4.3 copy-start.26
  595.2 46.2 %copy-start.21 = (f32[512]{0:T(512)S(1)}, f32[512]{0:T(512)}, u32[]{:S(2)}) copy-start(f32[512]{0:T(512)} %get-tuple-element.33) | copy-start | bytes 6148
  640.1 4.3 copy-start.27
  640.1 4.3 copy-start.28
  644.4 7.5 copy-start.19
  668.3 5.0 copy-start.13
  973.6 8.7 copy-start.11
  982.3 2.1 copy-start.14
  982.3 4.7 copy-start.1
  984.5 1.8 copy-start.15
Sparse Core Ops, SparseCore 0:
  653.2 315.7 all-reduce.15
where the time goes:
time: 1000 us; the launch traced here: 994 us
  blocking collectives  363 us (36%)
  waiting for transfers between devices  295 us (30%)
  local copies, waits for them, and re-layouts  158 us (16%)
  matrix products  83.9 us (8%)
  other arithmetic  79.1 us (8%)
  between operations  14.7 us (1%)
    psum x1, waiting for transfers between devices, local(): lax.psum((conv1_grad, conv2_grad, conv3_grad, head_grad, jigsaw_grad), 'i...  295 us
    psum x3, blocking collectives, statistics(): count, total = lax.psum((count_local, jnp.sum(value * mask, axis=0)), 'img')  122 us
    psum x3, blocking collectives, statistics(): spread = lax.psum(jnp.sum(centered * centered, axis=0), 'img') / count  121 us
    psum x3, blocking collectives, normalize_back(): lax.psum((jnp.sum(grad_norm, axis=0), jnp.sum(grad_norm * hat, axis=0)),...  120 us
    concatenate x9, local copies, waits for them, and re-layouts, gather_taps(): return jnp.concatenate(pieces, axis=-1).reshape(-1, 9 * width)  30.5 us
    reduce_sum x2, other arithmetic, normalize_back(): jnp.sum(grad_norm, axis=0)  27.7 us
    unnamed x74, local copies, waits for them, and re-layouts  23.7 us
  transfers between devices with their start and end apart: 1, of which 1 were waited for; matrix products, arithmetic and copies ran while one was open for 2% of the time, Pallas kernels for 0%

commit v1 on v0

v1 whole, which is shorter than its diff:
```python
import functools
import math

import jax
import jax.numpy as jnp
import numpy as np
from jax import lax
from jax.experimental import pallas as pl
from jax.experimental.pallas import tpu as pltpu
from jax.sharding import PartitionSpec as P

epsilon = 1e-05
f32 = jnp.float32
bf16 = jnp.bfloat16
TAPS = ((-1, -1), (-1, 0), (-1, 1), (0, -1), (0, 0), (0, 1), (1, -1), (1, 0), (1, 1))
VMEM_LIMIT = 56 * 1024 * 1024


def up(n, m):
    return (n + m - 1) // m * m


def tap_pairs(tap):
    dr, dc = TAPS[tap]
    pairs = []
    for r in range(3):
        for c in range(3):
            if 0 <= r + dr < 3 and 0 <= c + dc < 3:
                pairs.append((3 * r + c, 3 * (r + dr) + c + dc))
    return pairs


def needs_three(pixel):
    return max(pixel // 3, pixel % 3) == 2


def sigmoid(u):
    return 0.5 * jnp.tanh(0.5 * u) + 0.5


def wide(mask, width):
    return jnp.concatenate([mask] * (width // 128), axis=1)


def col8(v):
    return jnp.sum(v.reshape(v.shape[0] // 8, 8, v.shape[1]), axis=0)


def nt(a, b):
    return lax.dot_general(a, b, (((1,), (1,)), ((), ())), preferred_element_type=f32)


def tn(a, b):
    return lax.dot_general(a, b, (((0,), (0,)), ((), ())), preferred_element_type=f32)


def nn(a, b):
    return jnp.dot(a, b, preferred_element_type=f32)


def tile_masks(side_ref, mk_ref, images):
    rows = lax.broadcasted_iota(jnp.int32, mk_ref.shape[1:], 0)
    mk_ref[0] = jnp.where(rows < 9 * images, 1.0, 0.0).astype(f32)
    three = jnp.zeros(mk_ref.shape[1:], f32)
    for i in range(images):
        flag = jnp.where(side_ref[i] > 2, 1.0, 0.0).astype(f32)
        three = jnp.where((rows >= 9 * i) & (rows < 9 * i + 9), flag, three)
    mk_ref[1] = three


def pixel_mask(mk_ref, pixel, width):
    return wide(mk_ref[1 if needs_three(pixel) else 0], width)


def row_masks(side_ref, inner_ref, mk_ref, images):
    inner = inner_ref[...]
    mk_ref[80 * images :, :] = jnp.zeros((mk_ref.shape[0] - 80 * images, 128), f32)
    for i in range(images):
        flag = jnp.where(side_ref[i] > 2, 1.0, 0.0).astype(f32)
        mk_ref[80 * i : 80 * i + 80, :] = jnp.maximum(inner, flag)
        mk_ref[80 * images + i : 80 * images + i + 1, :] = jnp.full((1, 128), flag)


def take_rows(src_ref, dst_ref, last_ref, images):
    for i in range(images):
        dst_ref[80 * i : 80 * i + 80, :] = src_ref[i, 0:80, :]
        last_ref[i : i + 1, :] = src_ref[i, 80:81, :].astype(f32)
    dst_ref[80 * images :, :] = last_ref[...].astype(bf16)


def local_count(side_ref, images):
    total = 0
    for i in range(images):
        total = total + side_ref[i] * side_ref[i]
    return (9 * total).astype(f32)


def put(dense_ref, at, value):
    for n in range(dense_ref.shape[0]):
        dense_ref[n, at, :] = value[:, 128 * n : 128 * n + 128]


def get(dense_ref, at):
    return jnp.concatenate([dense_ref[n, at, :] for n in range(dense_ref.shape[0])], axis=1)


def pixel_rows(pixel, tiles):
    return pl.ds(pixel, tiles, stride=9)


def wide_to_dense(src_ref, dense_ref, images):
    for i in range(images):
        put(dense_ref, slice(81 * i, 81 * i + 80), src_ref[80 * i : 80 * i + 80, :])
        put(dense_ref, slice(81 * i + 80, 81 * i + 81), src_ref[80 * images + i : 80 * images + i + 1, :])
    tail = dense_ref.shape[1] - 81 * images
    if tail:
        put(dense_ref, slice(81 * images, None), jnp.zeros((tail, src_ref.shape[1]), f32))


def dense_to_wide(dense_ref, dst_ref, images):
    for i in range(images):
        dst_ref[80 * i : 80 * i + 80, :] = get(dense_ref, slice(81 * i, 81 * i + 80)).astype(bf16)
    last = [get(dense_ref, slice(81 * i + 80, 81 * i + 81)) for i in range(images)]
    last.append(jnp.zeros((dst_ref.shape[0] - 81 * images, dst_ref.shape[1]), f32))
    dst_ref[80 * images :, :] = jnp.concatenate(last, axis=0).astype(bf16)


def pixel_stats(pre_ref, mk_ref, count, tiles, width):
    acc = jnp.zeros((8, width), f32)
    for p in range(9):
        acc = acc + col8(pre_ref[p] * pixel_mask(mk_ref, p, width))
    mean = jnp.sum(acc, axis=0, keepdims=True) / count
    acc = jnp.zeros((8, width), f32)
    for p in range(9):
        centered = (pre_ref[p] - mean) * pixel_mask(mk_ref, p, width)
        acc = acc + col8(centered * centered)
    return mean, jnp.sum(acc, axis=0, keepdims=True)


def combine(stats, counts):
    width = stats.shape[2]
    n = jnp.concatenate([counts[:, 0:1, :]] * (width // 128), axis=2)
    means = stats[:, 0:1, :]
    total = jnp.sum(n, axis=0)
    mean = jnp.sum(n * means, axis=0) / total
    off = means - mean[None]
    spread = jnp.sum(stats[:, 1:2, :] + n * off * off, axis=0) / total
    return mean, lax.rsqrt(spread + epsilon), total


def conv1_kernel(images, devices, side_ref, x_ref, w_ref, pre_ref, st_ref, xs, last, acc, dense, mk):
    step = pl.program_id(0)
    tiles, width = pre_ref.shape[1], pre_ref.shape[2]

    @pl.when(step == 0)
    def _():
        last[...] = jnp.zeros_like(last)

    take_rows(x_ref, xs, last, images)

    @pl.when(step == 0)
    def _():
        acc[...] = nn(xs[...], w_ref[...])

    @pl.when(step > 0)
    def _():
        acc[...] += nn(xs[...], w_ref[...])

    @pl.when(step == pl.num_programs(0) - 1)
    def _():
        tile_masks(side_ref, mk, images)
        wide_to_dense(acc, dense, images)
        for p in range(9):
            value = get(dense, pixel_rows(p, tiles))
            if needs_three(p):
                value = value * pixel_mask(mk, p, width)
            pre_ref[p] = value
        count = local_count(side_ref, images)
        mean, spread = pixel_stats(pre_ref, mk, count, tiles, width)
        row = jnp.concatenate([mean, spread], axis=0)
        row = jnp.concatenate([row, jnp.full((2, 128), count)], axis=1)
        st_ref[...] = jnp.broadcast_to(row[None], st_ref.shape)


def norm_parts(stats_ref, counts_ref, bn_ref):
    mean, scale, total = combine(stats_ref[...], counts_ref[...])
    bn_ref[0:1, :] = mean
    bn_ref[1:2, :] = scale
    bn_ref[2:3, :] = total
    return mean, scale


def conv2_kernel(images, devices, side_ref, pre_ref, stats_ref, counts_ref, gain_ref, bias_ref, w_hbm, out_ref, st_ref, bn_ref, w, act, mk, sem):
    tiles, width = pre_ref.shape[1], pre_ref.shape[2]
    order = [4, 0, 1, 2, 3, 5, 6, 7, 8]
    copies = {k: pltpu.make_async_copy(w_hbm.at[k], w.at[k], sem.at[k]) for k in order}
    for k in order:
        copies[k].start()
    tile_masks(side_ref, mk, images)
    mean, scale = norm_parts(stats_ref, counts_ref, bn_ref)
    slope = scale * gain_ref[...]
    bias = bias_ref[...]
    for p in range(9):
        u = (pre_ref[p] - mean) * slope + bias
        act[p * tiles : (p + 1) * tiles, :] = (u * sigmoid(u) * pixel_mask(mk, p, width)).astype(bf16)
    for k in order:
        copies[k].wait()
        pairs = tap_pairs(k)
        lhs = jnp.concatenate([act[q * tiles : (q + 1) * tiles, :] for _, q in pairs], axis=0)
        r = nn(lhs, w[k])
        for n, (p, _) in enumerate(pairs):
            part = r[n * tiles : (n + 1) * tiles]
            if k == order[0]:
                out_ref[p] = part
            else:
                out_ref[p] += part
    count = local_count(side_ref, images)
    mean, spread = pixel_stats(out_ref, mk, count, tiles, width)
    row = jnp.concatenate([mean, spread], axis=0)
    st_ref[...] = jnp.broadcast_to(row[None], st_ref.shape)


def conv3_kernel(images, devices, side_ref, pre_ref, stats_ref, counts_ref, gain_ref, bias_ref, inner_ref, w_hbm, act_ref, st_ref, bn_ref, w, dense, pre, mk, rmk, sem):
    tiles, width = pre_ref.shape[1], pre_ref.shape[2]
    rows, channels = act_ref.shape[0], w.shape[1]
    copy = pltpu.make_async_copy(w_hbm, w, sem)
    copy.start()
    tile_masks(side_ref, mk, images)
    row_masks(side_ref, inner_ref, rmk, images)
    mean, scale = norm_parts(stats_ref, counts_ref, bn_ref)
    slope = scale * gain_ref[...]
    bias = bias_ref[...]
    for p in range(9):
        u = (pre_ref[p] - mean) * slope + bias
        put(dense, pixel_rows(p, tiles), u * sigmoid(u) * pixel_mask(mk, p, width))
    dense_to_wide(dense, act_ref, images)
    copy.wait()
    count = local_count(side_ref, images)
    part = 512
    for c in range(channels // part):
        cols = slice(c * part, (c + 1) * part)
        pre[...] = nn(act_ref[...], w[:, cols])
        acc = jnp.zeros((8, part), f32)
        for b in range(rows // 128):
            acc = acc + col8(pre[128 * b : 128 * b + 128, :])
        mean = jnp.sum(acc, axis=0, keepdims=True) / count
        acc = jnp.zeros((8, part), f32)
        for b in range(rows // 128):
            centered = (pre[128 * b : 128 * b + 128, :] - mean) * wide(rmk[128 * b : 128 * b + 128, :], part)
            acc = acc + col8(centered * centered)
        row = jnp.concatenate([mean, jnp.sum(acc, axis=0, keepdims=True)], axis=0)
        st_ref[:, :, cols] = jnp.broadcast_to(row[None], (devices, 2, part))


def head_kernel(
    images, side_ref, source_ref, act_ref, w_ref, stats_ref, counts_ref, gain_ref, bias_ref, x_ref, g_ref, head_ref, spread_ref, pool_ref, inner_ref, jc_ref, jw_ref,
    out_ref, sg_ref, sums_ref, bn_ref, emb_ref, hg_ref,
    xs, gs, last, lastg, pre, spr, os, lasto, rmk, area, tarea, jg, eg, egb, egr,
):
    step = pl.program_id(0)
    rows, part = xs.shape
    embed = head_ref.shape[1]
    main = 80 * images

    @pl.when(step == 0)
    def _():
        last[...] = jnp.zeros_like(last)
        lastg[...] = jnp.zeros_like(lastg)
        row_masks(side_ref, inner_ref, rmk, images)
        area[main:, :] = jnp.zeros((rows - main, 128), f32)
        tarea[...] = jnp.zeros_like(tarea)
        eg[...] = jnp.zeros_like(eg)
        for i in range(images):
            value = jnp.where(side_ref[i] > 2, 1.0 / 9.0, 0.25).astype(f32)
            area[80 * i : 80 * i + 80, :] = jnp.full((80, 128), value)
            area[main + i : main + i + 1, :] = jnp.full((1, 128), value)
            tarea[9 * i : 9 * i + 9, :] = jnp.full((9, 128), value)
        for k in range(9):
            jg[k] = nt(jc_ref[...], jw_ref[k * embed : (k + 1) * embed, :])
        for i in range(images):
            for k in range(9):
                place = 9 * i + lax.rem(source_ref[9 * i + k], 9)
                eg[pl.ds(place, 1), :] = jg[k, i : i + 1, :]
        egb[...] = eg[...].astype(bf16)
        egr[...] = nn(spread_ref[...], egb[...]).astype(bf16)
        emb_ref[...] = jnp.zeros_like(emb_ref)

    take_rows(x_ref, xs, last, images)
    take_rows(g_ref, gs, lastg, images)
    mean, scale, total = combine(stats_ref[...], counts_ref[...])
    bn_ref[0:1, :] = mean
    bn_ref[1:2, :] = scale
    bn_ref[2:3, :] = total
    pre[...] = nn(act_ref[...], w_ref[...])
    spr[...] = nt(egr[...], head_ref[...])
    gain, bias = gain_ref[...], bias_ref[...]
    acc_b = jnp.zeros((8, part), f32)
    acc_g = jnp.zeros((8, part), f32)
    for b in range(rows // 64):
        at = slice(64 * b, 64 * b + 64)
        hat = (pre[at, :] - mean) * scale
        u = hat * gain + bias + xs[at, :].astype(f32)
        s = sigmoid(u)
        us = u * s
        mask = wide(rmk[at, :], part)
        out = us * mask
        os[at, :] = out.astype(bf16)
        if 64 * b + 64 > main:
            lo = max(main - 64 * b, 0)
            lasto[64 * b + lo - main : 64 * b + 64 - main, :] = out[lo:]
        slope = s + us * (1.0 - s)
        sg = (gs[at, :].astype(f32) + wide(area[at, :], part) * spr[at, :]) * slope * mask
        sg_ref[at, :] = sg
        acc_b = acc_b + col8(sg)
        acc_g = acc_g + col8(sg * hat)
    sums_ref[0:1, :] = jnp.sum(acc_b, axis=0, keepdims=True)
    sums_ref[1:2, :] = jnp.sum(acc_g, axis=0, keepdims=True)
    for i in range(images):
        out_ref[i, 0:80, :] = os[80 * i : 80 * i + 80, :]
        out_ref[i, 80:81, :] = lasto[i : i + 1, :].astype(bf16)
    pooled = (nn(pool_ref[...], os[...]) * wide(tarea[...], part)).astype(bf16)
    emb_ref[...] += nn(pooled, head_ref[...])
    hg_ref[...] = tn(pooled, egb[...])


def jigsaw_kernel(images, source_ref, emb_ref, jc_ref, jw_ref, out_ref, jgrad_ref, emb, jn, jcp):
    embed = emb_ref.shape[1]
    emb[...] = emb_ref[...].astype(bf16).astype(f32)
    jn[...] = jnp.zeros_like(jn)
    jcp[...] = jnp.zeros_like(jcp)
    jcp[0:images, :] = jc_ref[...].astype(f32)
    for i in range(images):
        for k in range(9):
            place = 9 * i + lax.rem(source_ref[9 * i + k], 9)
            jn[k, i : i + 1, :] = emb[pl.ds(place, 1), :]
    total = jnp.zeros((jn.shape[1], embed), f32)
    jcv = jcp[...].astype(bf16)
    for k in range(9):
        value = jn[k].astype(bf16)
        total = total + nn(value, jw_ref[k * embed : (k + 1) * embed, :])
        jgrad_ref[k * embed : (k + 1) * embed, :] = tn(value, jcv)
    out_ref[...] = total[0:images]


def third_kernel(images, devices, side_ref, act_ref, w_ref, bn3_ref, gain3_ref, sums_ref, sg_ref, pre2_ref, bn2_ref, gain2_ref, bias2_ref, cg_ref, dy_ref, st_ref, actt, ds3, acc, dense, mk):
    step = pl.program_id(0)
    tiles, width = pre2_ref.shape[1], pre2_ref.shape[2]
    rows, part = sg_ref.shape

    @pl.when(step == 0)
    def _():
        actt[...] = act_ref[...].astype(f32).T.astype(bf16)
        acc[...] = jnp.zeros_like(acc)

    mean, scale, total = bn3_ref[0:1, :], bn3_ref[1:2, :], bn3_ref[2:3, :]
    lead = gain3_ref[...] * scale
    db = sums_ref[0:1, :] / total
    dg = sums_ref[1:2, :] / total
    pre = nn(act_ref[...], w_ref[...])
    hat = (pre - mean) * scale
    ds3[...] = (lead * (sg_ref[...] - db - hat * dg)).astype(bf16)
    cg_ref[...] = nn(actt[...], ds3[...])
    acc[...] += nt(ds3[...], w_ref[...])

    @pl.when(step == pl.num_programs(0) - 1)
    def _():
        tile_masks(side_ref, mk, images)
        wide_to_dense(acc, dense, images)
        mean2, scale2 = bn2_ref[0:1, :], bn2_ref[1:2, :]
        gain, bias = gain2_ref[...], bias2_ref[...]
        acc_b = jnp.zeros((8, width), f32)
        acc_g = jnp.zeros((8, width), f32)
        for p in range(9):
            hat2 = (pre2_ref[p] - mean2) * scale2
            u = hat2 * gain + bias
            s = sigmoid(u)
            slope = s + u * s * (1.0 - s)
            dy = get(dense, pixel_rows(p, tiles)) * slope * pixel_mask(mk, p, width)
            dy_ref[p] = dy
            acc_b = acc_b + col8(dy)
            acc_g = acc_g + col8(dy * hat2)
        row = jnp.concatenate([jnp.sum(acc_b, axis=0, keepdims=True), jnp.sum(acc_g, axis=0, keepdims=True)], axis=0)
        st_ref[...] = jnp.broadcast_to(row[None], st_ref.shape)


def norm_back(pre, dy, mean, scale, gain, db, dg, mask):
    hat = (pre - mean) * scale
    return (mask * (scale * gain)) * (dy - db - hat * dg)


def second_grad_kernel(images, side_ref, pre1_ref, bn1_ref, gain1_ref, bias1_ref, pre2_ref, bn2_ref, gain2_ref, dy_ref, sums_ref, cg_ref, d_ref, gb_ref, actt, mk):
    tap = pl.program_id(0)
    tiles, width = pre1_ref.shape[1], pre1_ref.shape[2]

    @pl.when(tap == 0)
    def _():
        tile_masks(side_ref, mk, images)
        sums = jnp.sum(sums_ref[...], axis=0)
        gb_ref[...] = sums
        db, dg = sums[0:1] / bn2_ref[2:3, :], sums[1:2] / bn2_ref[2:3, :]
        slope = bn1_ref[1:2, :] * gain1_ref[...]
        mean1, bias1 = bn1_ref[0:1, :], bias1_ref[...]
        mean2, scale2, gain2 = bn2_ref[0:1, :], bn2_ref[1:2, :], gain2_ref[...]
        for p in range(9):
            mask = pixel_mask(mk, p, width)
            d_ref[p] = norm_back(pre2_ref[p], dy_ref[p], mean2, scale2, gain2, db, dg, mask).astype(bf16)
            u = (pre1_ref[p] - mean1) * slope + bias1
            actt[:, p * tiles : (p + 1) * tiles] = (u * sigmoid(u) * mask).T.astype(bf16)

    for k in range(9):

        @pl.when(tap == k)
        def _():
            pairs = tap_pairs(k)
            lhs = jnp.concatenate([actt[:, q * tiles : (q + 1) * tiles] for _, q in pairs], axis=1)
            rhs = jnp.concatenate([d_ref[p] for p, _ in pairs], axis=0)
            cg_ref[...] = nn(lhs, rhs)


def second_back_kernel(images, devices, side_ref, d_ref, w_hbm, pre1_ref, bn1_ref, gain1_ref, bias1_ref, dy_ref, st_ref, w, acc, mk, sem):
    tiles, width = d_ref.shape[1], d_ref.shape[2]
    order = [4, 0, 1, 2, 3, 5, 6, 7, 8]
    copies = {k: pltpu.make_async_copy(w_hbm.at[k], w.at[k], sem.at[k]) for k in order}
    for k in order:
        copies[k].start()
    tile_masks(side_ref, mk, images)
    for k in order:
        copies[k].wait()
        pairs = tap_pairs(k)
        lhs = jnp.concatenate([d_ref[p] for p, _ in pairs], axis=0)
        r = nt(lhs, w[k])
        for n, (_, q) in enumerate(pairs):
            part = r[n * tiles : (n + 1) * tiles]
            if k == order[0]:
                acc[q] = part
            else:
                acc[q] += part
    mean, scale = bn1_ref[0:1, :], bn1_ref[1:2, :]
    gain, bias = gain1_ref[...], bias1_ref[...]
    acc_b = jnp.zeros((8, width), f32)
    acc_g = jnp.zeros((8, width), f32)
    for p in range(9):
        hat = (pre1_ref[p] - mean) * scale
        u = hat * gain + bias
        s = sigmoid(u)
        slope = s + u * s * (1.0 - s)
        dy = acc[p] * slope * pixel_mask(mk, p, width)
        dy_ref[p] = dy
        acc_b = acc_b + col8(dy)
        acc_g = acc_g + col8(dy * hat)
    row = jnp.concatenate([jnp.sum(acc_b, axis=0, keepdims=True), jnp.sum(acc_g, axis=0, keepdims=True)], axis=0)
    st_ref[...] = jnp.broadcast_to(row[None], st_ref.shape)


def first_kernel(images, side_ref, inner_ref, x_ref, w_ref, sg_ref, pre1_ref, bn1_ref, gain1_ref, dy_ref, sums_ref, cg_ref, out_ref, gb_ref, d, xs, last, dense, ig, mk, rmk):
    step = pl.program_id(0)
    tiles, width = pre1_ref.shape[1], pre1_ref.shape[2]
    rows, part = sg_ref.shape
    main = 80 * images

    @pl.when(step == 0)
    def _():
        last[...] = jnp.zeros_like(last)
        tile_masks(side_ref, mk, images)
        row_masks(side_ref, inner_ref, rmk, images)
        sums = jnp.sum(sums_ref[...], axis=0)
        gb_ref[...] = sums
        db, dg = sums[0:1] / bn1_ref[2:3, :], sums[1:2] / bn1_ref[2:3, :]
        mean, scale, gain = bn1_ref[0:1, :], bn1_ref[1:2, :], gain1_ref[...]
        for p in range(9):
            mask = pixel_mask(mk, p, width)
            put(dense, pixel_rows(p, tiles), norm_back(pre1_ref[p], dy_ref[p], mean, scale, gain, db, dg, mask))
        dense_to_wide(dense, d, images)

    take_rows(x_ref, xs, last, images)
    cg_ref[...] = tn(xs[...], d[...])
    ig[...] = (nt(d[...], w_ref[...]) + sg_ref[...]) * wide(rmk[...], part)
    for i in range(images):
        out_ref[i, 0:80, :] = ig[80 * i : 80 * i + 80, :].astype(bf16)
        out_ref[i, 80:81, :] = ig[main + i : main + i + 1, :].astype(bf16)


def params(semantics=None):
    return pltpu.CompilerParams(vmem_limit_bytes=VMEM_LIMIT, dimension_semantics=semantics)


def full(shape):
    return pl.BlockSpec(shape, lambda *_: (0,) * len(shape))


def call(kernel, grid, in_specs, out_specs, out_shape, scratch, prefetch, flops=0, moved=0):
    return pl.pallas_call(
        kernel,
        grid_spec=pltpu.PrefetchScalarGridSpec(
            num_scalar_prefetch=prefetch, grid=grid, in_specs=in_specs, out_specs=out_specs, scratch_shapes=scratch
        ),
        out_shape=out_shape,
        compiler_params=params(("arbitrary",) * len(grid)),
        cost_estimate=pl.CostEstimate(flops=flops, bytes_accessed=moved, transcendentals=0),
    )


def exchange(value):
    return lax.all_to_all(value, "img", 0, 0)


def bits_of(devices):
    return [1 << n for n in range(devices.bit_length() - 1)]


def swap(value, bit, devices):
    return lax.ppermute(value, "img", [(i, i ^ bit) for i in range(devices)])


def small_sum(value, devices):
    bits = bits_of(devices)
    groups = [[bits[0]]]
    rest = bits[1:]
    while rest:
        a = rest[:2]
        groups.append(a if len(a) == 1 else [a[0], a[1], a[0] | a[1]])
        rest = rest[2:]
    for group in groups:
        pieces = [swap(value, k, devices) for k in group]
        for piece in pieces:
            value = value + piece
    return value


def own_bit(bit):
    return (lax.axis_index("img") // bit) % 2


def part_of(v, n, size):
    return lax.dynamic_slice_in_dim(v, n * size, size, 0)


def halve(v, bit, devices):
    half = v.shape[0] // 2
    mine = own_bit(bit)
    return part_of(v, mine, half) + swap(part_of(v, 1 - mine, half), bit, devices)


def double(w, bit, devices):
    mine = own_bit(bit)
    other = swap(w, bit, devices)
    return jnp.concatenate([jnp.where(mine == 0, w, other), jnp.where(mine == 0, other, w)], axis=0)


def big_sum(v, devices):
    bits = bits_of(devices)
    v = halve(v, bits[0], devices)
    half = v.shape[0] // 2
    first, second = v[:half], v[half:]
    near = bits[1:]
    swapped = near[:2][::-1] + near[2:]
    for a, b in zip(near, swapped):
        first = halve(first, a, devices)
        second = halve(second, b, devices)
    for a, b in zip(near[::-1], swapped[::-1]):
        first = double(first, a, devices)
        second = double(second, b, devices)
    return double(jnp.concatenate([first, second], axis=0), bits[0], devices)


def local(devices, block_input, grid_side, tile_source, conv1_weight, gain1, bias1, conv2_weight, gain2, bias2, conv3_weight, gain3, bias3, head_weight, jigsaw_weight, out_cotangent, jigsaw_cotangent):
    images, slots, channels = block_input.shape
    neck, embed = conv1_weight.shape[1], head_weight.shape[1]
    rows = up(slots * images, 128)
    main = 80 * images
    tiles = up(9 * images, 16)
    dense_rows = 9 * tiles
    S = jax.ShapeDtypeStruct
    V = pltpu.VMEM
    any_spec = pl.BlockSpec(memory_space=pl.ANY)
    lines = lambda v: v.reshape(1, -1)
    gain1, bias1, gain2, bias2, gain3, bias3 = map(lines, (gain1, bias1, gain2, bias2, gain3, bias3))

    slot = np.arange(80)
    inner = ((slot % 9 // 3 < 2) & (slot % 3 < 2)).astype(np.float32)
    inner = jnp.asarray(np.repeat(inner[:, None], 128, axis=1))
    which = np.zeros((rows, tiles), np.float32)
    for i in range(images):
        for s in range(slots):
            which[80 * i + s if s < 80 else main + i, 9 * i + s // 9] = 1.0
    spread_mat = jnp.asarray(which, bf16)
    pool_mat = jnp.asarray(which.T.copy(), bf16)

    kc = 512
    pre1, st1 = call(
        functools.partial(conv1_kernel, images, devices),
        (channels // kc,),
        [pl.BlockSpec((images, slots, kc), lambda s, *_: (0, 0, s)), pl.BlockSpec((kc, neck), lambda s, *_: (s, 0))],
        [full((9, tiles, neck)), full((devices, 2, neck + 128))],
        [S((9, tiles, neck), f32), S((devices, 2, neck + 128), f32)],
        [V((rows, kc), bf16), V((rows - main, kc), f32), V((rows, neck), f32), V((neck // 128, dense_rows, 128), f32), V((2, tiles, 128), f32)],
        1,
    )(grid_side, block_input, conv1_weight)
    got1 = exchange(st1)
    counts = got1[:, :, neck:]
    stats1 = got1[:, :, :neck]

    pre2, st2, bn1 = call(
        functools.partial(conv2_kernel, images, devices),
        (1,),
        [full((9, tiles, neck)), full((devices, 2, neck)), full((devices, 2, 128)), full((1, neck)), full((1, neck)), any_spec],
        [full((9, tiles, neck)), full((devices, 2, neck)), full((8, neck))],
        [S((9, tiles, neck), f32), S((devices, 2, neck), f32), S((8, neck), f32)],
        [V((9, neck, neck), bf16), V((9 * tiles, neck), bf16), V((2, tiles, 128), f32), pltpu.SemaphoreType.DMA((9,))],
        1,
    )(grid_side, pre1, stats1, counts, gain1, bias1, conv2_weight)
    stats2 = exchange(st2)

    act2, st3, bn2 = call(
        functools.partial(conv3_kernel, images, devices),
        (1,),
        [full((9, tiles, neck)), full((devices, 2, neck)), full((devices, 2, 128)), full((1, neck)), full((1, neck)), full((80, 128)), any_spec],
        [full((rows, neck)), full((devices, 2, channels)), full((8, neck))],
        [S((rows, neck), bf16), S((devices, 2, channels), f32), S((8, neck), f32)],
        [V((neck, channels), bf16), V((neck // 128, dense_rows, 128), f32), V((rows, 512), f32), V((2, tiles, 128), f32), V((rows, 128), f32), pltpu.SemaphoreType.DMA],
        1,
    )(grid_side, pre2, stats2, counts, gain2, bias2, inner, conv3_weight)
    stats3 = exchange(st3)

    part = 256
    col = lambda s, *_: (0, s)
    col3 = lambda s, *_: (0, 0, s)
    row = lambda s, *_: (s, 0)
    block_output, sg, sums3, bn3, emb, head_grad = call(
        functools.partial(head_kernel, images),
        (channels // part,),
        [
            full((rows, neck)), pl.BlockSpec((neck, part), col), pl.BlockSpec((devices, 2, part), col3), full((devices, 2, 128)),
            pl.BlockSpec((1, part), col), pl.BlockSpec((1, part), col), pl.BlockSpec((images, slots, part), col3), pl.BlockSpec((images, slots, part), col3),
            pl.BlockSpec((part, embed), row), full((rows, tiles)), full((tiles, rows)), full((80, 128)), full((images, embed)), full((9 * embed, embed)),
        ],
        [
            pl.BlockSpec((images, slots, part), col3), pl.BlockSpec((rows, part), col), pl.BlockSpec((2, part), col), pl.BlockSpec((8, part), col),
            full((tiles, embed)), pl.BlockSpec((part, embed), row),
        ],
        [S(block_input.shape, bf16), S((rows, channels), f32), S((2, channels), f32), S((8, channels), f32), S((tiles, embed), f32), S((channels, embed), f32)],
        [
            V((rows, part), bf16), V((rows, part), bf16), V((rows - main, part), f32), V((rows - main, part), f32), V((rows, part), f32), V((rows, part), f32),
            V((rows, part), bf16), V((rows - main, part), f32), V((rows, 128), f32), V((rows, 128), f32), V((tiles, 128), f32),
            V((9, images, embed), f32), V((tiles, embed), f32), V((tiles, embed), bf16), V((rows, embed), bf16),
        ],
        2,
    )(grid_side, tile_source, act2, conv3_weight, stats3, counts, gain3, bias3, block_input, out_cotangent, head_weight, spread_mat, pool_mat, inner, jigsaw_cotangent, jigsaw_weight)
    sums3 = small_sum(sums3, devices)

    padded = up(images, 16)
    jigsaw_out, jigsaw_grad = call(
        functools.partial(jigsaw_kernel, images),
        (1,),
        [full((tiles, embed)), full((images, embed)), full((9 * embed, embed))],
        [full((images, embed)), full((9 * embed, embed))],
        [S((images, embed), f32), S((9 * embed, embed), f32)],
        [V((tiles, embed), f32), V((9, padded, embed), f32), V((padded, embed), f32)],
        1,
    )(tile_source, emb, jigsaw_cotangent, jigsaw_weight)
    sums3, jigsaw_grad, jigsaw_out = lax.optimization_barrier((sums3, jigsaw_grad, jigsaw_out))

    conv3_grad, dy2, st5 = call(
        functools.partial(third_kernel, images, devices),
        (channels // part,),
        [
            full((rows, neck)), pl.BlockSpec((neck, part), col), pl.BlockSpec((8, part), col), pl.BlockSpec((1, part), col), pl.BlockSpec((2, part), col),
            pl.BlockSpec((rows, part), col), full((9, tiles, neck)), full((8, neck)), full((1, neck)), full((1, neck)),
        ],
        [pl.BlockSpec((neck, part), col), full((9, tiles, neck)), full((devices, 2, neck))],
        [S((neck, channels), f32), S((9, tiles, neck), f32), S((devices, 2, neck), f32)],
        [V((neck, rows), bf16), V((rows, part), bf16), V((rows, neck), f32), V((neck // 128, dense_rows, 128), f32), V((2, tiles, 128), f32)],
        1,
    )(grid_side, act2, conv3_weight, bn3, gain3, sums3, sg, pre2, bn2, gain2, bias2)
    sums2 = exchange(st5)

    conv2_grad, d2, gb2 = call(
        functools.partial(second_grad_kernel, images),
        (9,),
        [full((9, tiles, neck)), full((8, neck)), full((1, neck)), full((1, neck)), full((9, tiles, neck)), full((8, neck)), full((1, neck)), full((9, tiles, neck)), full((devices, 2, neck))],
        [pl.BlockSpec((neck, neck), row), full((9, tiles, neck)), full((2, neck))],
        [S((9 * neck, neck), f32), S((9, tiles, neck), bf16), S((2, neck), f32)],
        [V((neck, 9 * tiles), bf16), V((2, tiles, 128), f32)],
        1,
    )(grid_side, pre1, bn1, gain1, bias1, pre2, bn2, gain2, dy2, sums2)

    dy1, st6 = call(
        functools.partial(second_back_kernel, images, devices),
        (1,),
        [full((9, tiles, neck)), any_spec, full((9, tiles, neck)), full((8, neck)), full((1, neck)), full((1, neck))],
        [full((9, tiles, neck)), full((devices, 2, neck))],
        [S((9, tiles, neck), f32), S((devices, 2, neck), f32)],
        [V((9, neck, neck), bf16), V((9, tiles, neck), f32), V((2, tiles, 128), f32), pltpu.SemaphoreType.DMA((9,))],
        1,
    )(grid_side, d2, conv2_weight, pre1, bn1, gain1, bias1)
    sums1 = exchange(st6)

    conv1_grad, input_grad, gb1 = call(
        functools.partial(first_kernel, images),
        (channels // part,),
        [
            full((80, 128)), pl.BlockSpec((images, slots, part), col3), pl.BlockSpec((part, neck), row), pl.BlockSpec((rows, part), col),
            full((9, tiles, neck)), full((8, neck)), full((1, neck)), full((9, tiles, neck)), full((devices, 2, neck)),
        ],
        [pl.BlockSpec((part, neck), row), pl.BlockSpec((images, slots, part), col3), full((2, neck))],
        [S((channels, neck), f32), S(block_input.shape, bf16), S((2, neck), f32)],
        [
            V((rows, neck), bf16), V((rows, part), bf16), V((rows - main, part), f32), V((neck // 128, dense_rows, 128), f32), V((rows, part), f32),
            V((2, tiles, 128), f32), V((rows, 128), f32),
        ],
        1,
    )(grid_side, inner, block_input, conv1_weight, sg, pre1, bn1, gain1, dy1, sums1)

    conv3_grad, head_grad, jigsaw_grad = lax.psum((conv3_grad, head_grad, jigsaw_grad), "img")
    conv2_grad = big_sum(conv2_grad, devices).reshape(9, neck, neck)
    conv1_grad = big_sum(conv1_grad, devices)
    return (
        block_output, jigsaw_out, input_grad, conv1_grad, gb1[1], gb1[0], conv2_grad, gb2[1], gb2[0], conv3_grad, sums3[1], sums3[0], head_grad, jigsaw_grad,
    )


def solution(mesh):
    devices = math.prod(mesh.shape.values())
    split3, split2, split1, whole = P("img", None, None), P("img", None), P("img"), P()
    return jax.shard_map(
        functools.partial(local, devices),
        mesh=mesh,
        in_specs=(split3, split1, split1) + (whole,) * 11 + (split3, split2),
        out_specs=(split3, split2, split3) + (whole,) * 11,
        check_vma=False,
    )
```

time: 1000 us -> 574 us (0.57)
  blocking collectives: 363 us -> 46.4 us
  local copies, waits for them, and re-layouts: 158 us -> 24.3 us
  Pallas kernels: 0 us -> 111 us
  matrix products: 83.9 us -> 0 us
  starting transfers between devices: 0.04 us -> 60.5 us
  other arithmetic: 79.1 us -> 28.5 us
  waiting for transfers between devices: 295 us -> 279 us
    psum x9 -> x0, blocking collectives: 363 us -> none  [the longest x3 122 us: statistics(): count, total = lax.psum((count_local, jnp.sum(value * mask, axis=0)), 'img')]
    psum x1, waiting for transfers between devices: 295 us -> 134 us  [local(): lax.psum((conv3_grad, head_grad, jigsaw_grad), 'img')]
    ppermute x0 -> x43, waiting for transfers between devices: none -> 134 us  [swap(): return lax.ppermute(value, 'img', [(i, i ^ bit) for i in range(devices)])]
    pallas_call x0 -> x9, Pallas kernels: none -> 111 us  [the longest x1 20.6 us: local(): call(functools.partial(third_kernel, images, devices), (channels // part,...]
    dot_general x15 -> x0, matrix products: 83.9 us -> none  [the longest x1 12.7 us: local(): jnp.einsum('rk,rm->km', columns, second_back, preferred_element_type=jnp....]
    ppermute x0 -> x43, starting transfers between devices: none -> 55 us  [swap(): return lax.ppermute(value, 'img', [(i, i ^ bit) for i in range(devices)])]
    reduce_sum x7 -> x0, other arithmetic: 47.1 us -> none  [the longest x2 27.7 us: normalize_back(): jnp.sum(grad_norm, axis=0)]
    all_to_all x0 -> x3, blocking collectives: none -> 46.4 us  [exchange(): return lax.all_to_all(value, 'img', 0, 0)]
  transfers between devices with their start and end apart: 1 -> 46, of which waited for: 1 -> 31; matrix products, arithmetic and copies ran while one was open for 2% -> 7% of each run, Pallas kernels for 0% -> 4%
where the time goes in v1:
time: 574 us; the launch traced here: 565 us
  waiting for transfers between devices  279 us (49%)
  Pallas kernels  111 us (19%)
  starting transfers between devices  60.5 us (11%)
  blocking collectives  46.4 us (8%)
  other arithmetic  28.5 us (5%)
  local copies, waits for them, and re-layouts  24.3 us (4%)
  between operations  15.2 us (3%)
    ppermute x43, waiting for transfers between devices, swap(): return lax.ppermute(value, 'img', [(i, i ^ bit) for i in range(devices)])  134 us
    psum x1, waiting for transfers between devices, local(): lax.psum((conv3_grad, head_grad, jigsaw_grad), 'img')  134 us
    ppermute x43, starting transfers between devices, swap(): return lax.ppermute(value, 'img', [(i, i ^ bit) for i in range(devices)])  55 us
    all_to_all x3, blocking collectives, exchange(): return lax.all_to_all(value, 'img', 0, 0)  46.4 us
    pallas_call x1, Pallas kernels, local(): call(functools.partial(third_kernel, images, devices), (channels // part,...  20.6 us
    pallas_call x1, Pallas kernels, local(): call(functools.partial(head_kernel, images), (channels // part,), [full((...  19.8 us
    pallas_call x1, Pallas kernels, local(): call(functools.partial(first_kernel, images), (channels // part,), [full(...  17.1 us
    pallas_call x1, Pallas kernels, local(): call(functools.partial(second_grad_kernel, images), (9,), [full((9, tiles...  13.2 us
  transfers between devices with their start and end apart: 46, of which 31 were waited for; matrix products, arithmetic and copies ran while one was open for 7% of the time, Pallas kernels for 4%

profile of v1, /device:TPU:0, one launch (start us, length us, event | category | flops | bytes accessed | tf_op | source)
XLA Modules:
  0.0 565.2 jit_solution(6690012345364306209)
XLA Ops:
  7.2 8.7 %shard_map.290 = (f32[9,128,512]{2,1,0:T(8,128)}, f32[32,2,640]{2,1,0:T(2,128)}) custom-call(s32[14]{0:T(128)} %side_ref.15, bf16[14,81,2048]{2,1,0:T(8,128)(2,1)} %x_ref.5, bf16[2048,512]{1,0:T(8,128)(2,1)} %w_ref.7), custom_call_target="tpu_custom_call" | custom-call | tf_op jit(solution)/shard_map/pallas_call | solution.py:590
  15.8 15.9 %all_to_all.25 = f32[32,2,640]{2,1,0:T(2,128)S(1)} all-to-all(f32[32,2,640]{2,1,0:T(2,128)} %get-tuple-element.45), channel_id=1, replica_groups=mesh['img'=32] {'img'}, dimensions={0} | all-to-all | bytes 327680 | tf_op jit(solution)/shard_map/all_to_all | solution.py:504
  33.0 9.6 %shard_map.291 = (f32[9,128,512]{2,1,0:T(8,128)}, f32[32,2,512]{2,1,0:T(2,128)}, f32[8,512]{1,0:T(8,128)}) custom-call(s32[14]{0:T(128)} %side_ref.15, f32[9,128,512]{2,1,0:T(8,128)} %get-tuple-element.44.pre_ref.pre1_ref, f32[32,2,512]{2,1,0:T(2,128)} %slice.48.stats_ref, f32[32,2,128]{2,1,0:T(2,128)} %slice.49.counts_ref, f32[1,512]{1,0:T(1,128)} %bitcast.16, ...), custom_call_target="tpu_custom_call" | custom-call | tf_op jit(solution)/shard_map/pallas_call | solution.py:603
  42.6 11.5 %all_to_all.26.stats_ref = f32[32,2,512]{2,1,0:T(2,128)} all-to-all(f32[32,2,512]{2,1,0:T(2,128)} %get-tuple-element.47), channel_id=1, replica_groups=mesh['img'=32] {'img'}, dimensions={0} | all-to-all | bytes 262144 | tf_op jit(solution)/shard_map/all_to_all | solution.py:504
  54.1 8.6 %shard_map.292 = (bf16[1152,512]{1,0:T(8,128)(2,1)}, f32[32,2,2048]{2,1,0:T(2,128)}, f32[8,512]{1,0:T(8,128)}) custom-call(s32[14]{0:T(128)} %side_ref.15, f32[9,128,512]{2,1,0:T(8,128)} %get-tuple-element.46.pre_ref.pre2_ref, f32[32,2,512]{2,1,0:T(2,128)} %all_to_all.26.stats_ref, f32[32,2,128]{2,1,0:T(2,128)} %slice.49.counts_ref, f32[1,512]{1,0:T(1,128)} %bitcast.20, ...), custom_call_target="tpu_custom_call" | custom-call | tf_op jit(solution)/shard_map/pallas_call | solution.py:614
  62.7 19.0 %all_to_all.27.stats_ref = f32[32,2,2048]{2,1,0:T(2,128)} all-to-all(f32[32,2,2048]{2,1,0:T(2,128)} %get-tuple-element.49), channel_id=1, replica_groups=mesh['img'=32] {'img'}, dimensions={0} | all-to-all | bytes 1048576 | tf_op jit(solution)/shard_map/all_to_all | solution.py:504
  81.8 19.8 %shard_map.293 = (bf16[14,81,2048]{2,1,0:T(8,128)(2,1)}, f32[1152,2048]{1,0:T(8,128)}, f32[2,2048]{1,0:T(2,128)}, f32[8,2048]{1,0:T(8,128)}, f32[128,128]{1,0:T(8,128)}, /*index=5*/f32[2048,128]{1,0:T(8,128)}) custom-call(s32[14]{0:T(128)} %side_ref.15, s32[126]{0:T(128)} %source_ref.3, bf16[1152,512]{1,0:T(8,128)(2,1)} %get-tuple-element.48.act_ref, ...), custom_call_target="tpu_custom_call" | custom-call | tf_op jit(solution)/shard_map/pallas_call | solution.py:629
  118.1 20.6 %shard_map.295 = (f32[512,2048]{1,0:T(8,128)}, f32[9,128,512]{2,1,0:T(8,128)}, f32[32,2,512]{2,1,0:T(2,128)}) custom-call(s32[14]{0:T(128)} %side_ref.15, bf16[1152,512]{1,0:T(8,128)(2,1)} %get-tuple-element.48.act_ref, bf16[512,2048]{1,0:T(8,128)(2,1)} %w_ref.6, f32[8,2048]{1,0:T(8,128)} %get-tuple-element.59.bn3_ref, f32[1,2048]{1,0:T(1,128)} %bitcast.15, ...), custom_call_target="tpu_custom_call" | custom-call | tf_op jit(solution)/shard_map/pallas_call | solution.py:663
  141.5 8.2 %all-to-all-done.3.sums_ref = f32[32,2,512]{2,1,0:T(2,128)S(1)} async-done(((f32[32,2,512]{2,1,0:T(2,128)}), f32[32,2,512]{2,1,0:T(2,128)S(1)}, u32[]{:S(2)}, u32[]{:S(2)}) %all-to-all-start.3) | async-done | bytes 131104 | tf_op jit(solution)/shard_map/all_to_all | solution.py:504
  150.4 13.2 %shard_map.296 = (f32[4608,512]{1,0:T(8,128)}, bf16[9,128,512]{2,1,0:T(8,128)(2,1)}, f32[2,512]{1,0:T(2,128)}) custom-call(s32[14]{0:T(128)} %side_ref.15, f32[9,128,512]{2,1,0:T(8,128)} %get-tuple-element.44.pre_ref.pre1_ref, f32[8,512]{1,0:T(8,128)} %get-tuple-element.57.bn1_ref, f32[1,512]{1,0:T(1,128)} %bitcast.17, f32[1,512]{1,0:T(1,128)} %bitcast.24, ...), custom_call_target="tpu_custom_call" | custom-call | tf_op jit(solution)/shard_map/pallas_call | solution.py:677
  163.5 10.8 %shard_map.297 = (f32[9,128,512]{2,1,0:T(8,128)}, f32[32,2,512]{2,1,0:T(2,128)}) custom-call(s32[14]{0:T(128)} %side_ref.15, bf16[9,128,512]{2,1,0:T(8,128)(2,1)} %get-tuple-element.63.d_ref, bf16[9,512,512]{2,1,0:T(8,128)(2,1)} %w_hbm.5, f32[9,128,512]{2,1,0:T(8,128)} %get-tuple-element.44.pre_ref.pre1_ref, f32[8,512]{1,0:T(8,128)} %get-tuple-element.57.bn1_ref, ...), custom_call_target="tpu_custom_call" | custom-call | tf_op jit(solution)/shard_map/pallas_call | solution.py:687
  177.0 5.0 constant_dynamic-slice_fusion.8
  185.8 17.1 %shard_map.298 = (f32[2048,512]{1,0:T(8,128)}, bf16[14,81,2048]{2,1,0:T(8,128)(2,1)}, f32[2,512]{1,0:T(2,128)}) custom-call(s32[14]{0:T(128)} %side_ref.15, f32[80,128]{1,0:T(8,128)} %constant.243.clone.inner_ref, bf16[14,81,2048]{2,1,0:T(8,128)(2,1)} %x_ref.5, bf16[2048,512]{1,0:T(8,128)(2,1)} %w_ref.7, f32[1152,2048]{1,0:T(8,128)} %get-tuple-element.56.sg_ref, ...), custom_call_target="tpu_custom_call" | custom-call | tf_op jit(solution)/shard_map/pallas_call | solution.py:698
  206.2 4.2 collective-permute-done.7
  215.7 12.0 %collective-permute-done.16 = f32[256,512]{1,0:T(8,128)S(1)} collective-permute-done((f32[256,512]{1,0:T(8,128)}, f32[256,512]{1,0:T(8,128)S(1)}, u32[]{:S(2)}, u32[]{:S(2)}) %collective-permute-start.16) | collective-permute-done | bytes 524320 | tf_op jit(solution)/shard_map/ppermute | solution.py:512
  230.4 5.0 collective-permute-done.17
  236.1 4.9 dynamic-slice_add_fusion
  251.7 16.0 %collective-permute-done.34 = f32[576,512]{1,0:T(8,128)S(1)} collective-permute-done((f32[576,512]{1,0:T(8,128)S(1)}, f32[576,512]{1,0:T(8,128)S(1)}, u32[]{:S(2)}, u32[]{:S(2)}) %collective-permute-start.34) | collective-permute-done | bytes 1179680 | tf_op jit(solution)/shard_map/ppermute | solution.py:512
  272.6 8.3 %collective-permute-done.35 = f32[288,512]{1,0:T(8,128)S(1)} collective-permute-done((f32[288,512]{1,0:T(8,128)S(1)}, f32[288,512]{1,0:T(8,128)S(1)}, u32[]{:S(2)}, u32[]{:S(2)}) %collective-permute-start.35) | collective-permute-done | bytes 589856 | tf_op jit(solution)/shard_map/ppermute | solution.py:512
  283.4 8.1 %collective-permute-done.36 = f32[144,512]{1,0:T(8,128)S(1)} collective-permute-done((f32[144,512]{1,0:T(8,128)S(1)}, f32[144,512]{1,0:T(8,128)S(1)}, u32[]{:S(2)}, u32[]{:S(2)}) %collective-permute-start.36) | collective-permute-done | bytes 294944 | tf_op jit(solution)/shard_map/ppermute | solution.py:512
  299.3 5.9 %collective-permute-done.37 = f32[72,512]{1,0:T(8,128)S(1)} collective-permute-done((f32[72,512]{1,0:T(8,128)S(1)}, f32[72,512]{1,0:T(8,128)S(1)}, u32[]{:S(2)}, u32[]{:S(2)}) %collective-permute-start.37) | collective-permute-done | bytes 147488 | tf_op jit(solution)/shard_map/ppermute | solution.py:512
  308.4 5.6 collective-permute-done.38
  319.0 4.6 collective-permute-done.39
  326.8 4.9 collective-permute-start.32
  333.8 4.8 collective-permute-start.41
  338.6 7.3 %collective-permute-done.32 = f32[288,512]{1,0:T(8,128)S(1)} collective-permute-done((f32[288,512]{1,0:T(8,128)S(1)}, f32[288,512]{1,0:T(8,128)S(1)}, u32[]{:S(2)}, u32[]{:S(2)}) %collective-permute-start.32) | collective-permute-done | bytes 589856 | tf_op jit(solution)/shard_map/ppermute | solution.py:512
  353.4 14.8 %collective-permute-done.41 = f32[576,512]{1,0:T(8,128)S(1)} collective-permute-done((f32[576,512]{1,0:T(8,128)S(1)}, f32[576,512]{1,0:T(8,128)S(1)}, u32[]{:S(2)}, u32[]{:S(2)}) %collective-permute-start.41) | collective-permute-done | bytes 1179680 | tf_op jit(solution)/shard_map/ppermute | solution.py:512
  376.6 6.9 %collective-permute-done.14 = f32[128,512]{1,0:T(8,128)S(1)} collective-permute-done((f32[128,512]{1,0:T(8,128)S(1)}, f32[128,512]{1,0:T(8,128)S(1)}, u32[]{:S(2)}, u32[]{:S(2)}) %collective-permute-start.14) | collective-permute-done | bytes 262176 | tf_op jit(solution)/shard_map/ppermute | solution.py:512
  383.9 10.4 %collective-permute-done.23 = f32[256,512]{1,0:T(8,128)S(1)} collective-permute-done((f32[256,512]{1,0:T(8,128)S(1)}, f32[256,512]{1,0:T(8,128)S(1)}, u32[]{:S(2)}, u32[]{:S(2)}) %collective-permute-start.23) | collective-permute-done | bytes 524320 | tf_op jit(solution)/shard_map/ppermute | solution.py:512
  412.3 4.9 pad_maximum_fusion
  417.2 133.7 %all-reduce.3.cloned.1.call-done = (f32[512,2048]{1,0:T(8,128)}, f32[2048,128]{1,0:T(8,128)}, f32[1152,128]{1,0:T(8,128)}) async-done(((f32[512,2048]{1,0:T(8,128)}, f32[2048,128]{1,0:T(8,128)}, f32[1152,128]{1,0:T(8,128)}), (f32[512,2048]{1,0:T(8,128)}, f32[2048,128]{1,0:T(8,128)}, f32[1152,128]{1,0:T(8,128)})) %all-reduce.3.cloned.1.call-update) | async-done | bytes 5832720 | tf_op jit(solution)/shard_map/psum | solution.py:714
  550.9 4.8 copy.36
  (186 shorter events, 115.2 us)
Async XLA Ops:
  138.7 11.0 %all-to-all-start.3 = ((f32[32,2,512]{2,1,0:T(2,128)}), f32[32,2,512]{2,1,0:T(2,128)S(1)}, u32[]{:S(2)}, u32[]{:S(2)}) async-start(f32[32,2,512]{2,1,0:T(2,128)} %get-tuple-element.62), calls=%async_computation.3 | async-start | bytes 262144 | tf_op jit(solution)/shard_map/all_to_all | solution.py:504
  174.3 10.8 %all-to-all-start.4 = ((f32[32,2,512]{2,1,0:T(2,128)}), f32[32,2,512]{2,1,0:T(2,128)S(1)}, u32[]{:S(2)}, u32[]{:S(2)}) async-start(f32[32,2,512]{2,1,0:T(2,128)} %get-tuple-element.65), calls=%async_computation.4 | async-start | bytes 262144 | tf_op jit(solution)/shard_map/all_to_all | solution.py:504
  176.9 373.9 %all-reduce.3.cloned.1.call-start = ((), (), s32[]{:S(2)}) async-start(), calls=%async_computation.5 | async-start | bytes 11665408 | tf_op jit(solution)/shard_map/psum | solution.py:714
  181.9 54.2 %collective-permute-start.25 = (f32[2304,512]{1,0:T(8,128)}, f32[2304,512]{1,0:T(8,128)}, u32[]{:S(2)}, u32[]{:S(2)}) collective-permute-start(f32[2304,512]{1,0:T(8,128)} %constant_dynamic-slice_fusion.8), channel_id=1, source_target_pairs={{0,1},{1,0},{2,3},{3,2},{4,5},{5,4},{6,7},{7,6},{8,9},{9,8},{10,11... | collective-permute-start | bytes 14155784 | tf_op jit(solution)/shard_map/ppermute | solution.py:512
  213.4 14.3 %collective-permute-start.16 = (f32[256,512]{1,0:T(8,128)}, f32[256,512]{1,0:T(8,128)S(1)}, u32[]{:S(2)}, u32[]{:S(2)}) collective-permute-start(f32[256,512]{1,0:T(8,128)} %constant_dynamic-slice_fusion.12), channel_id=1, source_target_pairs={{0,4},{1,5},{2,6},{3,7},{4,0},{5,1},{6,2},{7,3},{8,12},{9,13},{10,... | collective-permute-start | bytes 1572872 | tf_op jit(solution)/shard_map/ppermute | solution.py:512
  214.9 13.9 %collective-permute-start.8 = (f32[256,512]{1,0:T(8,128)}, f32[256,512]{1,0:T(8,128)S(1)}, u32[]{:S(2)}, u32[]{:S(2)}) collective-permute-start(f32[256,512]{1,0:T(8,128)} %constant_dynamic-slice_fusion.16), channel_id=1, source_target_pairs={{0,2},{1,3},{2,0},{3,1},{4,6},{5,7},{6,4},{7,5},{8,10},{9,11},{10,... | collective-permute-start | bytes 1572872 | tf_op jit(solution)/shard_map/ppermute | solution.py:512
  228.9 13.4 %collective-permute-start.9 = (f32[128,512]{1,0:T(8,128)S(1)}, f32[128,512]{1,0:T(8,128)S(1)}, u32[]{:S(2)}, u32[]{:S(2)}) collective-permute-start(f32[128,512]{1,0:T(8,128)S(1)} %constant_dynamic-slice_fusion.15), channel_id=1, source_target_pairs={{0,4},{1,5},{2,6},{3,7},{4,0},{5,1},{6,2},{7,3},{8,12},{9,13},{10,... | collective-permute-start | bytes 786440 | tf_op jit(solution)/shard_map/ppermute | solution.py:512
  235.5 9.3 %collective-permute-start.18 = (f32[64,512]{1,0:T(8,128)S(1)}, f32[64,512]{1,0:T(8,128)S(1)}, u32[]{:S(2)}, u32[]{:S(2)}) collective-permute-start(f32[64,512]{1,0:T(8,128)S(1)} %constant_dynamic-slice_fusion.10), channel_id=1, source_target_pairs={{0,8},{1,9},{2,10},{3,11},{4,12},{5,13},{6,14},{7,15},{8,0},{9,1},... | collective-permute-start | bytes 393224 | tf_op jit(solution)/shard_map/ppermute | solution.py:512
  241.6 26.0 %collective-permute-start.34 = (f32[576,512]{1,0:T(8,128)S(1)}, f32[576,512]{1,0:T(8,128)S(1)}, u32[]{:S(2)}, u32[]{:S(2)}) collective-permute-start(f32[576,512]{1,0:T(8,128)S(1)} %constant_dynamic-slice_fusion.3), channel_id=1, source_target_pairs={{0,4},{1,5},{2,6},{3,7},{4,0},{5,1},{6,2},{7,3},{8,12},{9,13},{10,... | collective-permute-start | bytes 3538952 | tf_op jit(solution)/shard_map/ppermute | solution.py:512
  242.5 26.5 %collective-permute-start.26 = (f32[576,512]{1,0:T(8,128)S(1)}, f32[576,512]{1,0:T(8,128)S(1)}, u32[]{:S(2)}, u32[]{:S(2)}) collective-permute-start(f32[576,512]{1,0:T(8,128)S(1)} %constant_dynamic-slice_fusion.7), channel_id=1, source_target_pairs={{0,2},{1,3},{2,0},{3,1},{4,6},{5,7},{6,4},{7,5},{8,10},{9,11},{10,... | collective-permute-start | bytes 3538952 | tf_op jit(solution)/shard_map/ppermute | solution.py:512
  244.9 26.3 %collective-permute-start.19 = (f32[32,512]{1,0:T(8,128)S(1)}, f32[32,512]{1,0:T(8,128)S(1)}, u32[]{:S(2)}, u32[]{:S(2)}) collective-permute-start(f32[32,512]{1,0:T(8,128)S(1)} %constant_dynamic-slice_fusion.9), channel_id=1, source_target_pairs={{0,16},{1,17},{2,18},{3,19},{4,20},{5,21},{6,22},{7,23},{8,24},{9,... | collective-permute-start | bytes 196616 | tf_op jit(solution)/shard_map/ppermute | solution.py:512
  248.5 83.2 %collective-permute-start.11 = (f32[32,512]{1,0:T(8,128)S(1)}, f32[32,512]{1,0:T(8,128)S(1)}, u32[]{:S(2)}, u32[]{:S(2)}) collective-permute-start(f32[32,512]{1,0:T(8,128)S(1)} %constant_dynamic-slice_fusion.13), channel_id=1, source_target_pairs={{0,16},{1,17},{2,18},{3,19},{4,20},{5,21},{6,22},{7,23},{8,24},{9,... | collective-permute-start | bytes 196616 | tf_op jit(solution)/shard_map/ppermute | solution.py:512
  268.0 12.9 %collective-permute-start.35 = (f32[288,512]{1,0:T(8,128)S(1)}, f32[288,512]{1,0:T(8,128)S(1)}, u32[]{:S(2)}, u32[]{:S(2)}) collective-permute-start(f32[288,512]{1,0:T(8,128)S(1)} %constant_dynamic-slice_fusion.2), channel_id=1, source_target_pairs={{0,2},{1,3},{2,0},{3,1},{4,6},{5,7},{6,4},{7,5},{8,10},{9,11},{10,... | collective-permute-start | bytes 1769480 | tf_op jit(solution)/shard_map/ppermute | solution.py:512
  269.3 13.2 %collective-permute-start.27 = (f32[288,512]{1,0:T(8,128)S(1)}, f32[288,512]{1,0:T(8,128)S(1)}, u32[]{:S(2)}, u32[]{:S(2)}) collective-permute-start(f32[288,512]{1,0:T(8,128)S(1)} %constant_dynamic-slice_fusion.6), channel_id=1, source_target_pairs={{0,4},{1,5},{2,6},{3,7},{4,0},{5,1},{6,2},{7,3},{8,12},{9,13},{10,... | collective-permute-start | bytes 1769480 | tf_op jit(solution)/shard_map/ppermute | solution.py:512
  271.1 75.1 %collective-permute-start.20 = (f32[32,512]{1,0:T(8,128)S(1)}, f32[32,512]{1,0:T(8,128)S(1)}, u32[]{:S(2)}, u32[]{:S(2)}) collective-permute-start(f32[32,512]{1,0:T(8,128)S(1)} %dynamic-slice_add_fusion.16), channel_id=1, source_target_pairs={{0,16},{1,17},{2,18},{3,19},{4,20},{5,21},{6,22},{7,23},{8,24},{9,... | collective-permute-start | bytes 196616 | tf_op jit(solution)/shard_map/ppermute | solution.py:512
  281.1 10.4 %collective-permute-start.36 = (f32[144,512]{1,0:T(8,128)S(1)}, f32[144,512]{1,0:T(8,128)S(1)}, u32[]{:S(2)}, u32[]{:S(2)}) collective-permute-start(f32[144,512]{1,0:T(8,128)S(1)} %constant_dynamic-slice_fusion.1), channel_id=1, source_target_pairs={{0,8},{1,9},{2,10},{3,11},{4,12},{5,13},{6,14},{7,15},{8,0},{9,1},... | collective-permute-start | bytes 884744 | tf_op jit(solution)/shard_map/ppermute | solution.py:512
  282.7 12.6 %collective-permute-start.28 = (f32[144,512]{1,0:T(8,128)S(1)}, f32[144,512]{1,0:T(8,128)S(1)}, u32[]{:S(2)}, u32[]{:S(2)}) collective-permute-start(f32[144,512]{1,0:T(8,128)S(1)} %constant_dynamic-slice_fusion.5), channel_id=1, source_target_pairs={{0,8},{1,9},{2,10},{3,11},{4,12},{5,13},{6,14},{7,15},{8,0},{9,1},... | collective-permute-start | bytes 884744 | tf_op jit(solution)/shard_map/ppermute | solution.py:512
  291.6 13.6 %collective-permute-start.37 = (f32[72,512]{1,0:T(8,128)S(1)}, f32[72,512]{1,0:T(8,128)S(1)}, u32[]{:S(2)}, u32[]{:S(2)}) collective-permute-start(f32[72,512]{1,0:T(8,128)S(1)} %constant_dynamic-slice_fusion), channel_id=1, source_target_pairs={{0,16},{1,17},{2,18},{3,19},{4,20},{5,21},{6,22},{7,23},{8,24},{9,... | collective-permute-start | bytes 442376 | tf_op jit(solution)/shard_map/ppermute | solution.py:512
  295.3 13.0 %collective-permute-start.29 = (f32[72,512]{1,0:T(8,128)S(1)}, f32[72,512]{1,0:T(8,128)S(1)}, u32[]{:S(2)}, u32[]{:S(2)}) collective-permute-start(f32[72,512]{1,0:T(8,128)S(1)} %constant_dynamic-slice_fusion.4), channel_id=1, source_target_pairs={{0,16},{1,17},{2,18},{3,19},{4,20},{5,21},{6,22},{7,23},{8,24},{9,... | collective-permute-start | bytes 442376 | tf_op jit(solution)/shard_map/ppermute | solution.py:512
  314.1 9.5 %collective-permute-start.39 = (f32[144,512]{1,0:T(8,128)S(1)}, f32[144,512]{1,0:T(8,128)S(1)}, u32[]{:S(2)}, u32[]{:S(2)}) collective-permute-start(f32[144,512]{1,0:T(8,128)S(1)} %pad_maximum_fusion.11), channel_id=1, source_target_pairs={{0,8},{1,9},{2,10},{3,11},{4,12},{5,13},{6,14},{7,15},{8,0},{9,1},... | collective-permute-start | bytes 884744 | tf_op jit(solution)/shard_map/ppermute | solution.py:512
  316.0 10.7 %collective-permute-start.31 = (f32[144,512]{1,0:T(8,128)S(1)}, f32[144,512]{1,0:T(8,128)S(1)}, u32[]{:S(2)}, u32[]{:S(2)}) collective-permute-start(f32[144,512]{1,0:T(8,128)S(1)} %pad_maximum_fusion.10), channel_id=1, source_target_pairs={{0,8},{1,9},{2,10},{3,11},{4,12},{5,13},{6,14},{7,15},{8,0},{9,1},... | collective-permute-start | bytes 884744 | tf_op jit(solution)/shard_map/ppermute | solution.py:512
  323.6 9.9 %collective-permute-start.40 = (f32[288,512]{1,0:T(8,128)S(1)}, f32[288,512]{1,0:T(8,128)S(1)}, u32[]{:S(2)}, u32[]{:S(2)}) collective-permute-start(f32[288,512]{1,0:T(8,128)S(1)} %pad_maximum_fusion.7), channel_id=1, source_target_pairs={{0,2},{1,3},{2,0},{3,1},{4,6},{5,7},{6,4},{7,5},{8,10},{9,11},{10,... | collective-permute-start | bytes 1769480 | tf_op jit(solution)/shard_map/ppermute | solution.py:512
  326.8 19.1 %collective-permute-start.32 = (f32[288,512]{1,0:T(8,128)S(1)}, f32[288,512]{1,0:T(8,128)S(1)}, u32[]{:S(2)}, u32[]{:S(2)}) collective-permute-start(f32[288,512]{1,0:T(8,128)S(1)} %pad_maximum_fusion.6), channel_id=1, source_target_pairs={{0,4},{1,5},{2,6},{3,7},{4,0},{5,1},{6,2},{7,3},{8,12},{9,13},{10,... | collective-permute-start | bytes 1769480 | tf_op jit(solution)/shard_map/ppermute | solution.py:512
  331.7 14.6 %collective-permute-start.12 = (f32[32,512]{1,0:T(8,128)S(1)}, f32[32,512]{1,0:T(8,128)S(1)}, u32[]{:S(2)}, u32[]{:S(2)}) collective-permute-start(f32[32,512]{1,0:T(8,128)S(1)} %dynamic-slice_add_fusion.17), channel_id=1, source_target_pairs={{0,16},{1,17},{2,18},{3,19},{4,20},{5,21},{6,22},{7,23},{8,24},{9,... | collective-permute-start | bytes 196616 | tf_op jit(solution)/shard_map/ppermute | solution.py:512
  333.8 34.4 %collective-permute-start.41 = (f32[576,512]{1,0:T(8,128)S(1)}, f32[576,512]{1,0:T(8,128)S(1)}, u32[]{:S(2)}, u32[]{:S(2)}) collective-permute-start(f32[576,512]{1,0:T(8,128)S(1)} %pad_maximum_fusion.5), channel_id=1, source_target_pairs={{0,4},{1,5},{2,6},{3,7},{4,0},{5,1},{6,2},{7,3},{8,12},{9,13},{10,... | collective-permute-start | bytes 3538952 | tf_op jit(solution)/shard_map/ppermute | solution.py:512
  346.1 24.9 %collective-permute-start.33 = (f32[576,512]{1,0:T(8,128)S(1)}, f32[576,512]{1,0:T(8,128)S(1)}, u32[]{:S(2)}, u32[]{:S(2)}) collective-permute-start(f32[576,512]{1,0:T(8,128)S(1)} %pad_maximum_fusion.4), channel_id=1, source_target_pairs={{0,2},{1,3},{2,0},{3,1},{4,6},{5,7},{6,4},{7,5},{8,10},{9,11},{10,... | collective-permute-start | bytes 3538952 | tf_op jit(solution)/shard_map/ppermute | solution.py:512
  346.4 27.9 %collective-permute-start.13 = (f32[64,512]{1,0:T(8,128)S(1)}, f32[64,512]{1,0:T(8,128)S(1)}, u32[]{:S(2)}, u32[]{:S(2)}) collective-permute-start(f32[64,512]{1,0:T(8,128)S(1)} %pad_maximum_fusion.14), channel_id=1, source_target_pairs={{0,8},{1,9},{2,10},{3,11},{4,12},{5,13},{6,14},{7,15},{8,0},{9,1},... | collective-permute-start | bytes 393224 | tf_op jit(solution)/shard_map/ppermute | solution.py:512
  351.4 24.5 %collective-permute-start.22 = (f32[128,512]{1,0:T(8,128)S(1)}, f32[128,512]{1,0:T(8,128)S(1)}, u32[]{:S(2)}, u32[]{:S(2)}) collective-permute-start(f32[128,512]{1,0:T(8,128)S(1)} %pad_maximum_fusion.13), channel_id=1, source_target_pairs={{0,2},{1,3},{2,0},{3,1},{4,6},{5,7},{6,4},{7,5},{8,10},{9,11},{10,... | collective-permute-start | bytes 786440 | tf_op jit(solution)/shard_map/ppermute | solution.py:512
  374.3 33.6 %collective-permute-start.42 = (f32[2304,512]{1,0:T(8,128)}, f32[2304,512]{1,0:T(8,128)}, u32[]{:S(2)}, u32[]{:S(2)}) collective-permute-start(f32[2304,512]{1,0:T(8,128)} %pad_maximum_fusion.1), channel_id=1, source_target_pairs={{0,1},{1,0},{2,3},{3,2},{4,5},{5,4},{6,7},{7,6},{8,9},{9,8},{10,11... | collective-permute-start | bytes 14155784 | tf_op jit(solution)/shard_map/ppermute | solution.py:512
  374.3 9.2 %collective-permute-start.14 = (f32[128,512]{1,0:T(8,128)S(1)}, f32[128,512]{1,0:T(8,128)S(1)}, u32[]{:S(2)}, u32[]{:S(2)}) collective-permute-start(f32[128,512]{1,0:T(8,128)S(1)} %pad_maximum_fusion.12), channel_id=1, source_target_pairs={{0,4},{1,5},{2,6},{3,7},{4,0},{5,1},{6,2},{7,3},{8,12},{9,13},{10,... | collective-permute-start | bytes 786440 | tf_op jit(solution)/shard_map/ppermute | solution.py:512
  376.0 18.4 %collective-permute-start.23 = (f32[256,512]{1,0:T(8,128)S(1)}, f32[256,512]{1,0:T(8,128)S(1)}, u32[]{:S(2)}, u32[]{:S(2)}) collective-permute-start(f32[256,512]{1,0:T(8,128)S(1)} %pad_maximum_fusion.9), channel_id=1, source_target_pairs={{0,4},{1,5},{2,6},{3,7},{4,0},{5,1},{6,2},{7,3},{8,12},{9,13},{10,... | collective-permute-start | bytes 1572872 | tf_op jit(solution)/shard_map/ppermute | solution.py:512
  383.6 13.2 %collective-permute-start.15 = (f32[256,512]{1,0:T(8,128)S(1)}, f32[256,512]{1,0:T(8,128)S(1)}, u32[]{:S(2)}, u32[]{:S(2)}) collective-permute-start(f32[256,512]{1,0:T(8,128)S(1)} %pad_maximum_fusion.8), channel_id=1, source_target_pairs={{0,2},{1,3},{2,0},{3,1},{4,6},{5,7},{6,4},{7,5},{8,10},{9,11},{10,... | collective-permute-start | bytes 1572872 | tf_op jit(solution)/shard_map/ppermute | solution.py:512
  (29 other events, 111.1 us)
Sparse Core Ops, SparseCore 0:
  398.6 152.2 all-reduce.2
